TPU v7x, 256 devices: a whole 4x4x8 slice. The times are simulated.
256 devices in a mesh: panel: 64 (over y, x, z_lo), slab: 4 (over z_hi, core).
Axes of the slice: x: 4, y: 4, z: 8 (z_hi: 2, z_lo: 4; z = z_hi * 4 + z_lo), core: 2. Of those that a mesh axis runs over, the one named last changes fastest.
Arguments:
- clip_cache: float32 [1024, 8192], P(None, 'panel'), may hold values from -6 to 6
- dose_scale: float32 [16, 8192], P(None, 'panel'), may hold values from 0.3 to 3
- focus_term: float32 [8, 8192], P(None, 'panel'), may hold values from -3 to 3
- clip_ids: int32 [32768], P('slab'), may hold values from 0 to 1023
- dose_ids: int32 [32768], P('slab'), may hold values from 0 to 15
- focus_ids: int32 [32768], P('slab'), may hold values from 0 to 7
Outputs:
- rotated: float32 [32768, 8192], P('slab', 'panel')
All inputs are finite; a program needn't handle non-finite values.
Results may differ from a plain program's by a relative error of at most 0.0001.
Values sent between devices are 32-bit elements; how exact they have to be, the bound alone decides.
A program may use at most 64 MiB of HBM per device.

v0:
```python
import jax
import jax.numpy as jnp
from jax import lax
from jax.sharding import PartitionSpec as P

ROUNDS = 2
EPSILON = 1e-06


def from_behind(block, axis, distance):
    devices = range(lax.axis_size(axis))
    route = [((i - distance) % len(devices), i) for i in devices]
    return lax.ppermute(block, axis, route)


def from_partner(value, axis, distance):
    mask = 2**distance
    pairs = [(source, source ^ mask) for source in range(lax.axis_size(axis))]
    return lax.ppermute(value, axis, pairs)


def block_rotation(gram):
    doubled = gram.shape[0]
    half_size = doubled // 2
    diagonal = jnp.diagonal(gram)
    coupling = gram / (diagonal[:, None] + diagonal[None, :])
    positions = lax.iota(jnp.int32, doubled)
    upper_mask = (positions[:, None] < half_size) & (positions[None, :] >= half_size)
    lower_mask = (positions[:, None] >= half_size) & (positions[None, :] < half_size)
    generator = 0.5 * (jnp.where(upper_mask, coupling, 0.0) - jnp.where(lower_mask, coupling, 0.0))
    identity = jnp.eye(doubled, dtype=gram.dtype)
    plus_half = identity + generator
    symmetric = identity + jnp.dot(
        generator.T, generator, precision=lax.Precision.HIGHEST, preferred_element_type=jnp.float32
    )
    factor = jnp.linalg.cholesky(symmetric)
    numerator = jnp.dot(
        plus_half, plus_half, precision=lax.Precision.HIGHEST, preferred_element_type=jnp.float32
    )
    return jax.scipy.linalg.cho_solve((factor, True), numerator)


def lookup(table_rows, indices):
    positions = lax.iota(jnp.int32, table_rows.shape[0])
    one_hot = (positions[:, None] == indices[None, :]).astype(jnp.float32)
    return lax.dot_general(
        one_hot,
        table_rows,
        (((0,), (0,)), ((), ())),
        precision=lax.Precision.HIGHEST,
        preferred_element_type=jnp.float32,
    )


def slab_gram(pair_block):
    gram_local = lax.dot_general(
        pair_block,
        pair_block,
        (((0,), (0,)), ((), ())),
        precision=lax.Precision.HIGHEST,
        preferred_element_type=jnp.float32,
    )
    return lax.psum(gram_local, "slab")


def product(left_side, right_side):
    return jnp.dot(
        left_side, right_side, precision=lax.Precision.HIGHEST, preferred_element_type=jnp.float32
    )


def shards(clip_cache, dose_scale, focus_term, clip_ids, dose_ids, focus_ids):
    row_count = clip_ids.shape[0]
    total_rows = row_count * lax.axis_size("slab")
    panel_width = clip_cache.shape[1]
    dose_part = lookup(dose_scale, dose_ids)
    focus_part = lookup(focus_term, focus_ids)
    jacobian = jnp.take(clip_cache, clip_ids, axis=0) * dose_part + focus_part
    col_squares = lax.psum(jnp.sum(jacobian * jacobian, axis=0), "slab")
    jacobian = jacobian * (1.0 / jnp.sqrt(col_squares / total_rows + EPSILON))
    seat_index = lax.axis_index("panel")
    is_odd = seat_index % 2 == 1
    own_start = seat_index % 2 * panel_width
    current = jacobian
    for section in range(ROUNDS):
        if section > 0:
            current = from_behind(current, "panel", 1)
        partner = from_partner(current, "panel", 0)
        pair_block = jnp.where(
            is_odd,
            jnp.concatenate([partner, current], axis=1),
            jnp.concatenate([current, partner], axis=1),
        )
        rotation = block_rotation(slab_gram(pair_block))
        own_cols = lax.dynamic_slice_in_dim(rotation, own_start, panel_width, 1)
        current = product(pair_block, own_cols)
    return current


def solution(mesh):
    return jax.shard_map(
        shards,
        mesh=mesh,
        in_specs=(
            P(None, "panel"),
            P(None, "panel"),
            P(None, "panel"),
            P("slab"),
            P("slab"),
            P("slab"),
        ),
        out_specs=P("slab", "panel"),
        check_vma=False,
    )
```

profile of v0, /device:TPU:1, one launch (start us, length us, event | category | flops | bytes accessed | tf_op | source)
XLA Modules:
  0.0 656.2 jit_solution(8444615578186647330)
XLA Ops:
  6.5 0.8 fusion.42
  7.4 0.8 compare_and_fusion
  8.2 28.0 %gather_fusion = f32[8192,128]{1,0:T(8,128)} fusion(f32[1024,128]{1,0:T(8,128)S(1)} %copy-done, s32[8192]{0:T(1024)S(1)} %fusion.42), kind=kCustom, calls=%fused_computation | custom fusion | bytes 8421376 | tf_op jit(solution)/shard_map/jit(_take)/gather | solution.py:78
  36.1 5.7 copy.15
  41.8 4.2 convolution_multiply_fusion
  46.0 4.2 multiply_reduce_fusion
  50.2 12.1 %psum.21 = f32[128]{0:T(128)S(1)} all-reduce(f32[128]{0:T(128)S(1)} %get-tuple-element.51), channel_id=1, replica_groups=mesh['panel'=64,'slab'=4] {'slab'}, use_global_device_ids=true, to_apply=%region_1.2 | all-reduce | flops 128 | bytes 1024 | tf_op jit(solution)/shard_map/psum | solution.py:79
  62.3 4.7 broadcast_multiply_fusion
  67.0 0.7 collective-permute-start
  67.7 85.9 %collective-permute-done = f32[8192,128]{0,1:T(8,128)} collective-permute-done((f32[8192,128]{0,1:T(8,128)}, f32[8192,128]{0,1:T(8,128)}, u32[]{:S(2)}, u32[]{:S(2)}) %collective-permute-start) | collective-permute-done | bytes 4194336 | tf_op jit(solution)/shard_map/ppermute | solution.py:19
  153.5 15.8 %fusion.3 = f32[256,256]{0,1:T(8,128)} fusion(f32[8192,128]{0,1:T(8,128)} %broadcast_multiply_fusion, f32[8192,128]{0,1:T(8,128)} %collective-permute-done, pred[]{:T(512)S(6)} %eq.42), kind=kOutput, calls=%fused_computation.14 | convolution fusion | flops 6448742400 | bytes 8650753 | tf_op jit(solution)/shard_map/dot_general | solution.py:56
  169.4 0.2 all-reduce.6.cloned.1.call-start
  169.6 62.4 %all-reduce.4.cloned.1.call-done = f32[256,256]{0,1:T(8,128)} async-done(((f32[256,256]{0,1:T(8,128)}), f32[256,256]{0,1:T(8,128)}) %all-reduce.4.cloned.1.call-update) | async-done | bytes 262160 | tf_op jit(solution)/shard_map/psum | solution.py:63
  232.0 2.7 gather_fusion.1
  234.7 1.6 convolution_add_fusion.2
  236.5 11.7 %cholesky.130 = f32[128,128]{1,0:T(8,128)S(1)} custom-call(f32[128,128]{1,0:T(8,128)S(1)} %cholesky.194), custom_call_target="Cholesky" | custom-call | tf_op jit(solution)/shard_map/jit(cholesky)/cholesky | solution.py:36
  248.3 9.8 %custom-call.19 = f32[1,128,128]{1,2,0:T(8,128)S(1)} custom-call(f32[1,128,128]{2,1,0:T(8,128)S(1)} %get-tuple-element.50), custom_call_target="InvertDiagBlocksLowerTriangular" | custom-call | tf_op jit(solution)/shard_map/jit(cholesky)/cholesky | solution.py:36
  258.1 0.2 constant_dynamic-update-slice_fusion.1
  258.3 0.3 convolution_subtract_fusion.5
  258.6 11.7 %cholesky.147 = f32[128,128]{1,0:T(8,128)S(1)} custom-call(f32[128,128]{1,0:T(8,128)S(1)} %convolution_subtract_fusion.5), custom_call_target="Cholesky" | custom-call | tf_op jit(solution)/shard_map/jit(cholesky)/cholesky | solution.py:36
  270.3 0.7 compare_reduce_fusion.2
  271.1 0.6 compare_reduce_fusion.3
  273.1 4.2 while.4
  273.3 0.6 fusion.73
  273.9 1.4 bitcast_dynamic-update-slice_fusion.4
  275.3 0.6 fusion.73
  275.9 1.4 bitcast_dynamic-update-slice_fusion.4
  277.3 19.7 %custom-call.20 = f32[2,128,128]{1,2,0:T(8,128)S(1)} custom-call(f32[2,128,128]{2,1,0:T(8,128)S(1)} %get-tuple-element.21), custom_call_target="InvertDiagBlocksLowerTriangular" | custom-call | tf_op jit(solution)/shard_map/jit(_cho_solve)/triangular_solve | solution.py:40
  297.0 0.8 fusion.12
  297.8 0.3 fusion.23
  298.1 0.3 convolution_subtract_fusion.3
  298.4 0.3 fusion.34
  298.7 0.3 fusion.33
  299.0 0.3 convolution_subtract_fusion.2
  299.3 0.3 fusion.32
  299.6 8.8 %fusion.2 = f32[8192,128]{0,1:T(8,128)S(1)} fusion(f32[8192,128]{0,1:T(8,128)} %broadcast_multiply_fusion, f32[8192,128]{0,1:T(8,128)} %collective-permute-done, pred[]{:T(512)S(6)} %eq.42, s32[]{:T(128)S(6)} %select_n.63, f32[128,256]{1,0:T(8,128)S(1)} %fusion.32, f32[128,256]{1,0:T(8,128)S(1)} %fusion.33), kind=kOutput, calls=%fused_computation.13 | convolution fusion | flops 3227549696 | bytes 12845061 | tf_op jit(solution)/shard_map/dot_general | solution.py:67
  308.4 98.5 %collective-permute-done.1 = f32[8192,128]{0,1:T(8,128)S(1)} collective-permute-done((f32[8192,128]{0,1:T(8,128)S(1)}, f32[8192,128]{0,1:T(8,128)S(1)}, u32[]{:S(2)}, u32[]{:S(2)}) %collective-permute-start.1) | collective-permute-done | bytes 4194336 | tf_op jit(solution)/shard_map/ppermute | solution.py:13
  406.9 1.9 copy-done.7
  408.8 91.7 %collective-permute-done.2 = f32[8192,128]{0,1:T(8,128)} collective-permute-done((f32[8192,128]{0,1:T(8,128)S(1)}, f32[8192,128]{0,1:T(8,128)}, u32[]{:S(2)}, u32[]{:S(2)}) %collective-permute-start.2) | collective-permute-done | bytes 4194336 | tf_op jit(solution)/shard_map/ppermute | solution.py:19
  500.5 15.4 %fusion.1 = f32[256,256]{0,1:T(8,128)} fusion(f32[8192,128]{0,1:T(8,128)} %copy-done.7, f32[8192,128]{0,1:T(8,128)} %collective-permute-done.2, pred[]{:T(512)S(6)} %eq.42), kind=kOutput, calls=%fused_computation.12 | convolution fusion | flops 6448742400 | bytes 8650753 | tf_op jit(solution)/shard_map/dot_general | solution.py:56
  516.0 47.7 %all-reduce.6.cloned.1.call-done = f32[256,256]{0,1:T(8,128)} async-done(((f32[256,256]{0,1:T(8,128)}), f32[256,256]{0,1:T(8,128)}) %all-reduce.6.cloned.1.call-update) | async-done | bytes 262160 | tf_op jit(solution)/shard_map/psum | solution.py:63
  563.7 2.7 gather_fusion.2
  566.4 1.6 convolution_add_fusion.1
  568.3 11.7 %cholesky.164 = f32[128,128]{1,0:T(8,128)S(1)} custom-call(f32[128,128]{1,0:T(8,128)S(1)} %cholesky.197), custom_call_target="Cholesky" | custom-call | tf_op jit(solution)/shard_map/jit(cholesky)/cholesky | solution.py:36
  580.0 9.8 %custom-call.21 = f32[1,128,128]{1,2,0:T(8,128)S(1)} custom-call(f32[1,128,128]{2,1,0:T(8,128)S(1)} %get-tuple-element.46), custom_call_target="InvertDiagBlocksLowerTriangular" | custom-call | tf_op jit(solution)/shard_map/jit(cholesky)/cholesky | solution.py:36
  589.8 0.2 constant_dynamic-update-slice_fusion
  590.1 0.3 convolution_subtract_fusion.4
  590.3 11.7 %cholesky.181 = f32[128,128]{1,0:T(8,128)S(1)} custom-call(f32[128,128]{1,0:T(8,128)S(1)} %convolution_subtract_fusion.4), custom_call_target="Cholesky" | custom-call | tf_op jit(solution)/shard_map/jit(cholesky)/cholesky | solution.py:36
  602.1 0.6 compare_reduce_fusion
  602.7 0.6 compare_reduce_fusion.1
  604.6 3.8 while.5
  604.6 0.6 fusion.74
  605.2 1.3 bitcast_dynamic-update-slice_fusion.5
  606.6 0.6 fusion.74
  607.1 1.3 bitcast_dynamic-update-slice_fusion.5
  608.5 19.8 %custom-call.22 = f32[2,128,128]{1,2,0:T(8,128)S(1)} custom-call(f32[2,128,128]{2,1,0:T(8,128)S(1)} %get-tuple-element.22), custom_call_target="InvertDiagBlocksLowerTriangular" | custom-call | tf_op jit(solution)/shard_map/jit(_cho_solve)/triangular_solve | solution.py:40
  628.3 0.8 fusion.13
  629.2 0.3 fusion.21
  629.5 0.3 convolution_subtract_fusion.1
  629.8 0.3 fusion.37
  630.1 0.3 fusion.36
  630.3 0.3 convolution_subtract_fusion
  630.7 0.3 fusion.35
  630.9 18.2 %fusion = f32[8192,128]{1,0:T(8,128)} fusion(f32[8192,128]{0,1:T(8,128)} %copy-done.7, f32[8192,128]{0,1:T(8,128)} %collective-permute-done.2, pred[]{:T(512)S(6)} %eq.42, s32[]{:T(128)S(6)} %select_n.63, f32[128,256]{1,0:T(8,128)S(1)} %fusion.35, f32[128,256]{1,0:T(8,128)S(1)} %fusion.36), kind=kOutput, calls=%fused_computation.11 | convolution fusion | flops 3227549696 | bytes 12845061 | tf_op jit(solution)/shard_map/dot_general | solution.py:67
  (45 shorter events, 0.9 us)
Async XLA Ops:
  6.5 1.6 copy-start
  6.5 225.5 %all-reduce.4.cloned.1.call-start = ((), (), s32[]{:S(2)}) async-start(), calls=%async_computation | async-start | bytes 524288 | tf_op jit(solution)/shard_map/psum | solution.py:63
  36.1 5.7 copy-start.3
  36.1 5.7 copy-start.5
  41.8 4.2 copy-start.4
  41.8 4.2 copy-start.6
  67.0 86.5 %collective-permute-start = (f32[8192,128]{0,1:T(8,128)}, f32[8192,128]{0,1:T(8,128)}, u32[]{:S(2)}, u32[]{:S(2)}) collective-permute-start(f32[8192,128]{0,1:T(8,128)} %broadcast_multiply_fusion), channel_id=1, source_target_pairs={{0,4},{4,0},{8,12},{12,8},{16,20},{20,16},{24,28},{28,24},{32,36},... | collective-permute-start | bytes 12582920 | tf_op jit(solution)/shard_map/ppermute | solution.py:19
  169.4 394.4 %all-reduce.6.cloned.1.call-start = ((), (), s32[]{:S(2)}) async-start(), calls=%async_computation.1 | async-start | bytes 524288 | tf_op jit(solution)/shard_map/psum | solution.py:63
  232.0 65.0 %copy-start.1 = (f32[256,256]{0,1:T(8,128)S(1)}, f32[256,256]{0,1:T(8,128)}, u32[]{:S(2)}) copy-start(f32[256,256]{0,1:T(8,128)} %all-reduce.4.cloned.1.call-done) | copy-start | bytes 786436
  308.3 98.6 %collective-permute-start.1 = (f32[8192,128]{0,1:T(8,128)S(1)}, f32[8192,128]{0,1:T(8,128)S(1)}, u32[]{:S(2)}, u32[]{:S(2)}) collective-permute-start(f32[8192,128]{0,1:T(8,128)S(1)} %fusion.2), channel_id=1, source_target_pairs={{252,0},{0,4},{4,8},{8,12},{12,16},{16,20},{20,24},{24,28},{28,32}... | collective-permute-start | bytes 12582920 | tf_op jit(solution)/shard_map/ppermute | solution.py:13
  406.9 1.9 copy-start.7
  408.8 91.7 %collective-permute-start.2 = (f32[8192,128]{0,1:T(8,128)S(1)}, f32[8192,128]{0,1:T(8,128)}, u32[]{:S(2)}, u32[]{:S(2)}) collective-permute-start(f32[8192,128]{0,1:T(8,128)S(1)} %collective-permute-done.1), channel_id=1, source_target_pairs={{0,4},{4,0},{8,12},{12,8},{16,20},{20,16},{24,28},{28,24},{32,36},... | collective-permute-start | bytes 12582920 | tf_op jit(solution)/shard_map/ppermute | solution.py:19
  563.7 64.6 %copy-start.2 = (f32[256,256]{0,1:T(8,128)S(1)}, f32[256,256]{0,1:T(8,128)}, u32[]{:S(2)}) copy-start(f32[256,256]{0,1:T(8,128)} %all-reduce.6.cloned.1.call-done) | copy-start | bytes 786436
Sparse Core Ops, SparseCore 0:
  169.5 62.4 all-reduce.3
  516.1 47.5 all-reduce.5
where the time goes:
time: 663 us; the launch traced here: 656 us
  waiting for transfers between devices  386 us (58%)
  other arithmetic  115 us (17%)
  matrix products  75.9 us (11%)
  local copies, waits for them, and re-layouts  49 us (7%)
  between operations  16.5 us (2%)
  blocking collectives  12.1 us (2%)
    ppermute x2, waiting for transfers between devices, from_partner(): return lax.ppermute(value, axis, pairs)  178 us
    psum x2, waiting for transfers between devices, slab_gram(): return lax.psum(gram_local, 'slab')  110 us
    ppermute x1, waiting for transfers between devices, from_behind(): return lax.ppermute(block, axis, route)  98.5 us
    another operation x14, other arithmetic, block_rotation(): factor = jnp.linalg.cholesky(symmetric)  69.2 us
    another operation x5, other arithmetic, block_rotation(): return jax.scipy.linalg.cho_solve((factor, True), numerator)  39.6 us
    gather x2, local copies, waits for them, and re-layouts, shards(): jacobian = jnp.take(clip_cache, clip_ids, axis=0) * dose_part + focus_part  33.6 us
    dot_general x2, matrix products, slab_gram(): lax.dot_general(pair_block, pair_block, (((0,), (0,)), ((), ())), precisi...  31.2 us
    dot_general x2, matrix products, product(): jnp.dot(left_side, right_side, precision=lax.Precision.HIGHEST, preferred...  27 us
  transfers between devices with their start and end apart: 5, of which 5 were waited for; matrix products, arithmetic and copies ran while one was open for 0% of the time, Pallas kernels for 0%

commit v1 on v0

--- a/solution.py
+++ b/solution.py
@@ -60,7 +60,7 @@
         precision=lax.Precision.HIGHEST,
         preferred_element_type=jnp.float32,
     )
-    return lax.psum(gram_local, "slab")
+    return jnp.sum(lax.all_gather(gram_local, "slab"), axis=0)
 
 
 def product(left_side, right_side):

time: 663 us -> 619 us (0.934)
  waiting for transfers between devices: 386 us -> 341 us
    psum x2 -> x0, waiting for transfers between devices: 110 us -> none  [slab_gram(): return lax.psum(gram_local, 'slab')]
    all_gather x0 -> x2, waiting for transfers between devices: none -> 65.9 us  [slab_gram(): return jnp.sum(lax.all_gather(gram_local, 'slab'), axis=0)]
where the time goes in v1:
time: 619 us; the launch traced here: 612 us
  waiting for transfers between devices  341 us (55%)
  other arithmetic  118 us (19%)
  matrix products  74.3 us (12%)
  local copies, waits for them, and re-layouts  49.1 us (8%)
  between operations  16.4 us (3%)
  blocking collectives  12.1 us (2%)
    ppermute x2, waiting for transfers between devices, from_partner(): return lax.ppermute(value, axis, pairs)  177 us
    ppermute x1, waiting for transfers between devices, from_behind(): return lax.ppermute(block, axis, route)  97.6 us
    another operation x14, other arithmetic, block_rotation(): factor = jnp.linalg.cholesky(symmetric)  69.2 us
    all_gather x2, waiting for transfers between devices, slab_gram(): return jnp.sum(lax.all_gather(gram_local, 'slab'), axis=0)  65.9 us
    another operation x5, other arithmetic, block_rotation(): return jax.scipy.linalg.cho_solve((factor, True), numerator)  39.8 us
    gather x2, local copies, waits for them, and re-layouts, shards(): jacobian = jnp.take(clip_cache, clip_ids, axis=0) * dose_part + focus_part  33.6 us
    dot_general x2, matrix products, slab_gram(): lax.dot_general(pair_block, pair_block, (((0,), (0,)), ((), ())), precisi...  31.7 us
    dot_general x2, matrix products, product(): jnp.dot(left_side, right_side, precision=lax.Precision.HIGHEST, preferred...  27 us
  transfers between devices with their start and end apart: 5, of which 5 were waited for; matrix products, arithmetic and copies ran while one was open for 0% of the time, Pallas kernels for 0%

profile of v1, /device:TPU:1, one launch (start us, length us, event | category | flops | bytes accessed | tf_op | source)
XLA Modules:
  0.0 611.7 jit_solution(7579337594691621368)
XLA Ops:
  6.5 0.8 fusion.42
  7.4 0.8 compare_and_fusion
  8.2 28.0 %gather_fusion = f32[8192,128]{1,0:T(8,128)} fusion(f32[1024,128]{1,0:T(8,128)S(1)} %copy-done, s32[8192]{0:T(1024)S(1)} %fusion.42), kind=kCustom, calls=%fused_computation | custom fusion | bytes 8421376 | tf_op jit(solution)/shard_map/jit(_take)/gather | solution.py:78
  36.1 5.7 copy.29
  41.8 4.2 convolution_multiply_fusion
  46.0 4.2 multiply_reduce_fusion
  50.2 12.1 %psum.7 = f32[128]{0:T(128)S(1)} all-reduce(f32[128]{0:T(128)S(1)} %get-tuple-element.51), channel_id=1, replica_groups=mesh['panel'=64,'slab'=4] {'slab'}, use_global_device_ids=true, to_apply=%region_1.2 | all-reduce | flops 128 | bytes 1024 | tf_op jit(solution)/shard_map/psum | solution.py:79
  62.3 4.7 broadcast_multiply_fusion
  67.0 0.7 collective-permute-start
  67.7 85.9 %collective-permute-done = f32[8192,128]{0,1:T(8,128)} collective-permute-done((f32[8192,128]{0,1:T(8,128)}, f32[8192,128]{0,1:T(8,128)}, u32[]{:S(2)}, u32[]{:S(2)}) %collective-permute-start) | collective-permute-done | bytes 4194336 | tf_op jit(solution)/shard_map/ppermute | solution.py:19
  153.5 16.7 %fusion.3 = f32[256,256]{1,0:T(8,128)} fusion(f32[8192,128]{0,1:T(8,128)} %broadcast_multiply_fusion, f32[8192,128]{0,1:T(8,128)} %collective-permute-done, pred[]{:T(512)S(6)} %eq.42), kind=kOutput, calls=%fused_computation.14 | convolution fusion | flops 6448742400 | bytes 8650753 | tf_op jit(solution)/shard_map/dot_general | solution.py:56
  170.3 39.5 %all-gather.5.cloned.1.call-done = f32[1024,256]{1,0:T(8,128)} async-done(((f32[256,256]{1,0:T(8,128)}), f32[1024,256]{1,0:T(8,128)}) %all-gather.5.cloned.1.call-update) | async-done | bytes 1048592 | tf_op jit(solution)/shard_map/all_gather | solution.py:63
  209.9 1.3 reduce_sum.28
  211.3 2.5 gather_fusion.1
  213.9 0.6 convolution_add_fusion.2
  214.5 0.8 fusion.12
  215.5 11.7 %cholesky.130 = f32[128,128]{1,0:T(8,128)S(1)} custom-call(f32[128,128]{1,0:T(8,128)S(1)} %cholesky.194), custom_call_target="Cholesky" | custom-call | tf_op jit(solution)/shard_map/jit(cholesky)/cholesky | solution.py:36
  227.3 9.8 %custom-call.19 = f32[1,128,128]{1,2,0:T(8,128)S(1)} custom-call(f32[1,128,128]{2,1,0:T(8,128)S(1)} %get-tuple-element.50), custom_call_target="InvertDiagBlocksLowerTriangular" | custom-call | tf_op jit(solution)/shard_map/jit(cholesky)/cholesky | solution.py:36
  237.3 0.3 convolution_subtract_fusion.5
  237.6 11.7 %cholesky.147 = f32[128,128]{1,0:T(8,128)S(1)} custom-call(f32[128,128]{1,0:T(8,128)S(1)} %convolution_subtract_fusion.5), custom_call_target="Cholesky" | custom-call | tf_op jit(solution)/shard_map/jit(cholesky)/cholesky | solution.py:36
  249.4 0.7 compare_reduce_fusion.2
  250.0 0.6 compare_reduce_fusion.3
  252.0 3.9 while.4
  252.0 0.6 fusion.73
  252.6 1.3 bitcast_dynamic-update-slice_fusion.4
  254.0 0.6 fusion.73
  254.6 1.3 bitcast_dynamic-update-slice_fusion.4
  255.9 19.9 %custom-call.20 = f32[2,128,128]{1,2,0:T(8,128)S(1)} custom-call(f32[2,128,128]{2,1,0:T(8,128)S(1)} %get-tuple-element.21), custom_call_target="InvertDiagBlocksLowerTriangular" | custom-call | tf_op jit(solution)/shard_map/jit(_cho_solve)/triangular_solve | solution.py:40
  275.8 0.3 fusion.23
  276.1 0.3 convolution_subtract_fusion.3
  276.4 0.3 fusion.34
  276.7 0.3 fusion.33
  277.0 0.3 convolution_subtract_fusion.2
  277.3 0.3 fusion.32
  277.6 8.8 %fusion.2 = f32[8192,128]{0,1:T(8,128)S(1)} fusion(f32[8192,128]{0,1:T(8,128)} %broadcast_multiply_fusion, f32[8192,128]{0,1:T(8,128)} %collective-permute-done, pred[]{:T(512)S(6)} %eq.42, s32[]{:T(128)S(6)} %select_n.63, f32[128,256]{1,0:T(8,128)S(1)} %fusion.32, f32[128,256]{1,0:T(8,128)S(1)} %fusion.33), kind=kOutput, calls=%fused_computation.13 | convolution fusion | flops 3227549696 | bytes 12845061 | tf_op jit(solution)/shard_map/dot_general | solution.py:67
  286.4 0.4 collective-permute-start.1
  286.8 97.6 %collective-permute-done.1 = f32[8192,128]{0,1:T(8,128)S(1)} collective-permute-done((f32[8192,128]{0,1:T(8,128)S(1)}, f32[8192,128]{0,1:T(8,128)S(1)}, u32[]{:S(2)}, u32[]{:S(2)}) %collective-permute-start.1) | collective-permute-done | bytes 4194336 | tf_op jit(solution)/shard_map/ppermute | solution.py:13
  384.4 1.9 copy-done.5
  386.3 91.1 %collective-permute-done.2 = f32[8192,128]{0,1:T(8,128)} collective-permute-done((f32[8192,128]{0,1:T(8,128)S(1)}, f32[8192,128]{0,1:T(8,128)}, u32[]{:S(2)}, u32[]{:S(2)}) %collective-permute-start.2) | collective-permute-done | bytes 4194336 | tf_op jit(solution)/shard_map/ppermute | solution.py:19
  477.4 15.0 %fusion.1 = f32[256,256]{1,0:T(8,128)} fusion(f32[8192,128]{0,1:T(8,128)} %copy-done.5, f32[8192,128]{0,1:T(8,128)} %collective-permute-done.2, pred[]{:T(512)S(6)} %eq.42), kind=kOutput, calls=%fused_computation.12 | convolution fusion | flops 6448742400 | bytes 8650753 | tf_op jit(solution)/shard_map/dot_general | solution.py:56
  492.4 26.4 %all-gather.7.cloned.1.call-done = f32[1024,256]{1,0:T(8,128)} async-done(((f32[256,256]{1,0:T(8,128)}), f32[1024,256]{1,0:T(8,128)}) %all-gather.7.cloned.1.call-update) | async-done | bytes 1048592 | tf_op jit(solution)/shard_map/all_gather | solution.py:63
  518.8 1.3 reduce_sum.29
  520.3 2.7 gather_fusion.2
  523.0 0.6 convolution_add_fusion.1
  523.6 0.8 fusion.13
  524.7 11.7 %cholesky.164 = f32[128,128]{1,0:T(8,128)S(1)} custom-call(f32[128,128]{1,0:T(8,128)S(1)} %cholesky.197), custom_call_target="Cholesky" | custom-call | tf_op jit(solution)/shard_map/jit(cholesky)/cholesky | solution.py:36
  536.5 9.8 %custom-call.21 = f32[1,128,128]{1,2,0:T(8,128)S(1)} custom-call(f32[1,128,128]{2,1,0:T(8,128)S(1)} %get-tuple-element.46), custom_call_target="InvertDiagBlocksLowerTriangular" | custom-call | tf_op jit(solution)/shard_map/jit(cholesky)/cholesky | solution.py:36
  546.5 0.3 convolution_subtract_fusion.4
  546.8 11.7 %cholesky.181 = f32[128,128]{1,0:T(8,128)S(1)} custom-call(f32[128,128]{1,0:T(8,128)S(1)} %convolution_subtract_fusion.4), custom_call_target="Cholesky" | custom-call | tf_op jit(solution)/shard_map/jit(cholesky)/cholesky | solution.py:36
  558.5 0.6 compare_reduce_fusion
  559.1 0.6 compare_reduce_fusion.1
  561.0 3.8 while.5
  561.1 0.6 fusion.74
  561.6 1.3 bitcast_dynamic-update-slice_fusion.5
  563.0 0.6 fusion.74
  563.6 1.3 bitcast_dynamic-update-slice_fusion.5
  564.9 19.8 %custom-call.22 = f32[2,128,128]{1,2,0:T(8,128)S(1)} custom-call(f32[2,128,128]{2,1,0:T(8,128)S(1)} %get-tuple-element.22), custom_call_target="InvertDiagBlocksLowerTriangular" | custom-call | tf_op jit(solution)/shard_map/jit(_cho_solve)/triangular_solve | solution.py:40
  584.7 0.3 fusion.21
  585.1 0.3 convolution_subtract_fusion.1
  585.3 0.3 fusion.37
  585.6 0.3 fusion.36
  585.9 0.3 convolution_subtract_fusion
  586.2 0.3 fusion.35
  586.5 18.2 %fusion = f32[8192,128]{1,0:T(8,128)} fusion(f32[8192,128]{0,1:T(8,128)} %copy-done.5, f32[8192,128]{0,1:T(8,128)} %collective-permute-done.2, pred[]{:T(512)S(6)} %eq.42, s32[]{:T(128)S(6)} %select_n.63, f32[128,256]{1,0:T(8,128)S(1)} %fusion.35, f32[128,256]{1,0:T(8,128)S(1)} %fusion.36), kind=kOutput, calls=%fused_computation.11 | convolution fusion | flops 3227549696 | bytes 12845061 | tf_op jit(solution)/shard_map/dot_general | solution.py:67
  (45 shorter events, 1.5 us)
Async XLA Ops:
  6.5 1.6 copy-start
  6.5 203.3 %all-gather.5.cloned.1.call-start = ((), (), s32[]{:S(2)}) async-start(), calls=%async_computation | async-start | bytes 1310720 | tf_op jit(solution)/shard_map/all_gather | solution.py:63
  36.1 5.7 copy-start.1
  36.1 5.7 copy-start.3
  41.8 4.2 copy-start.2
  41.8 4.2 copy-start.4
  67.0 86.5 %collective-permute-start = (f32[8192,128]{0,1:T(8,128)}, f32[8192,128]{0,1:T(8,128)}, u32[]{:S(2)}, u32[]{:S(2)}) collective-permute-start(f32[8192,128]{0,1:T(8,128)} %broadcast_multiply_fusion), channel_id=1, source_target_pairs={{0,4},{4,0},{8,12},{12,8},{16,20},{20,16},{24,28},{28,24},{32,36},... | collective-permute-start | bytes 12582920 | tf_op jit(solution)/shard_map/ppermute | solution.py:19
  170.3 348.5 %all-gather.7.cloned.1.call-start = ((), (), s32[]{:S(2)}) async-start(), calls=%async_computation.1 | async-start | bytes 1310720 | tf_op jit(solution)/shard_map/all_gather | solution.py:63
  286.4 98.0 %collective-permute-start.1 = (f32[8192,128]{0,1:T(8,128)S(1)}, f32[8192,128]{0,1:T(8,128)S(1)}, u32[]{:S(2)}, u32[]{:S(2)}) collective-permute-start(f32[8192,128]{0,1:T(8,128)S(1)} %fusion.2), channel_id=1, source_target_pairs={{252,0},{0,4},{4,8},{8,12},{12,16},{16,20},{20,24},{24,28},{28,32}... | collective-permute-start | bytes 12582920 | tf_op jit(solution)/shard_map/ppermute | solution.py:13
  384.4 1.9 copy-start.5
  386.3 91.1 %collective-permute-start.2 = (f32[8192,128]{0,1:T(8,128)S(1)}, f32[8192,128]{0,1:T(8,128)}, u32[]{:S(2)}, u32[]{:S(2)}) collective-permute-start(f32[8192,128]{0,1:T(8,128)S(1)} %collective-permute-done.1), channel_id=1, source_target_pairs={{0,4},{4,0},{8,12},{12,8},{16,20},{20,16},{24,28},{28,24},{32,36},... | collective-permute-start | bytes 12582920 | tf_op jit(solution)/shard_map/ppermute | solution.py:19
Sparse Core Ops, SparseCore 0:
  170.4 39.4 all-gather.4
  492.5 26.2 all-gather.6
